TPU v7x, 32 devices: a whole 2x2x4 slice. The times are simulated.
32 devices in a mesh: tower: 2 (over core), dp: 16 (over z, y, x).
Axes of the slice: x: 2, y: 2, z: 4, core: 2. Of those that a mesh axis runs over, the one named last changes fastest.
Arguments:
- latent: bfloat16 [32768, 256], P('dp'), may hold values from -6 to 6
- codes: int32 [2, 32768], P('tower', 'dp'), may hold values from 0 to 31, as said below
- targets: int32 [2, 3, 32768], P('tower', None, 'dp'), may hold values from 0 to 600, as said below
- visits: int32 [2, 32768, 4], P('tower', 'dp'), may hold values from 1 to 64
- importance: int32 [32768], P('dp'), may hold values from 1 to 1536
- params: float32 [2, 1054464], P('tower', 'dp'), as said below
- first_moment: float32 [2, 1054464], P('tower', 'dp')
- second_moment: float32 [2, 1054464], P('tower', 'dp'), as said below
Outputs:
- states: bfloat16 [2, 32768, 256], P('tower', 'dp')
- input_grad: float32 [2, 32768, 256], P('tower', 'dp')
- new_first: float32 [2, 1054464], P('tower', 'dp')
- new_second: float32 [2, 1054464], P('tower', 'dp')
- new_params: float32 [2, 1054464], P('tower', 'dp')
- params_low: bfloat16 [2, 1054464], P('tower', 'dp')
- norms: float32 [2, 2, 12], P('tower')
Inputs may be any that keep to these rules, and one draw needn't show every extreme that they name: codes[0] holds actions below 4, codes[1] chance codes. targets[t, 2] lies below 32. `params`: flat master parameters in the stated layout. `second_moment`: positive.
All inputs are finite; a program needn't handle non-finite values.
Results may differ from a plain program's by a relative error of at most 0.01.
The roundings to bfloat16 on the way count: a program that leaves them out, or rounds other values in their place, can miss the bound.
Values may be sent and summed in bfloat16 or wider, within the bound.
A program may use at most 320 MiB of HBM per device.

v0:
```python
import functools

import jax
import jax.numpy as jnp
from jax import lax
from jax.experimental import pallas as pl
from jax.experimental.pallas import tpu as pltpu
from jax.sharding import PartitionSpec as P

D = 256
CODES = 32
BINS = 601
BLOCKS = 10
STEP = 5
HEADS = 1238
MATS = 12
P_SIZE = 1054464
HPAD = 1280
CAT = D + CODES
A_ROWS = CAT + BLOCKS * D
BF = jnp.bfloat16
F32 = jnp.float32
GELU_C = 0.7978845608028654
GELU_K = 0.044715


def nn(a, b):
    return jnp.dot(a, b, preferred_element_type=F32)


def nt(a, b):
    return lax.dot_general(a, b, (((1,), (1,)), ((), ())), preferred_element_type=F32)


def identity(n):
    return (lax.broadcasted_iota(jnp.int32, (n, n), 0) == lax.broadcasted_iota(jnp.int32, (n, n), 1)).astype(BF)


ZETA = (GELU_C * GELU_K) ** (1.0 / 3.0)
B0 = GELU_C / ZETA
E0 = 0.5 / ZETA


def wide(v, cs):
    return jnp.concatenate([v] * ((cs.stop - cs.start) // v.shape[1]), 1)


def norm_act(src, cs, gs, unit, gp, rstd, out):
    for r in range(0, D, 32):
        rs = slice(r, r + 32)
        xh = src[rs, cs] * rstd
        z = xh * wide(gs[rs, 0:128], cs) + wide(gs[rs, 128:256], cs)
        z2 = z * z
        t = jnp.tanh(z * (z2 + B0))
        q = t * E0 + E0
        a = z * q
        out(rs, a)
        unit[rs, cs] = xh.astype(BF)
        gp[rs, cs] = (q + (a * (1.0 - t)) * (z2 * 3.0 + B0)).astype(BF)


def broadcast_vectors(vt, rows):
    k = lax.broadcasted_iota(jnp.int32, (128, 128), 0)
    picks = jnp.concatenate([(k == row).astype(BF) for row in rows], 1)
    return nn(vt, picks)


def head_stage(cs, lg, dl, ints, rw):
    width = rw.shape[1]
    it8 = lax.broadcasted_iota(jnp.int32, (8, width), 0)
    low = -jnp.inf
    b75, b150, b154 = lg[600:608], lg[1200:1208], lg[1232:1240]

    def top(block):
        return jnp.max(block, axis=0, keepdims=True)

    def steps(lo, hi, step):
        return [(r, min(r + step, hi)) for r in range(lo, hi, step)]

    def folded(value):
        return value.reshape(-1, 8, width)

    def top_range(lo, hi):
        best = None
        for r, end in steps(lo, hi, 40):
            part = jnp.max(folded(lg[r:end]), axis=0)
            best = part if best is None else jnp.maximum(best, part)
        return best

    max_v = top(jnp.maximum(top_range(0, 600), jnp.where(it8 < 1, b75, low)))
    max_r = top(
        jnp.maximum(
            jnp.maximum(top_range(608, 1200), jnp.where(it8 >= 1, b75, low)),
            jnp.where(it8 < 2, b150, low),
        )
    )
    max_c = top(
        jnp.maximum(
            jnp.maximum(top_range(1208, 1232), jnp.where(it8 >= 2, b150, low)),
            jnp.where(it8 < 2, b154, low),
        )
    )
    in_policy = (it8 >= 2) & (it8 < 6)
    max_p = top(jnp.where(in_policy, b154, low))

    def exp_range(lo, hi, best):
        acc = jnp.zeros((8, width), F32)
        for r, end in steps(lo, hi, 40):
            e = jnp.exp(lg[r:end] - best)
            lg[r:end] = e
            acc = acc + jnp.sum(folded(e), axis=0)
        return acc

    e75 = jnp.exp(b75 - jnp.where(it8 < 1, max_v, max_r))
    e150 = jnp.exp(b150 - jnp.where(it8 < 2, max_r, max_c))
    e154 = jnp.exp(b154 - jnp.where(it8 < 2, max_c, max_p))

    def total(acc):
        return rw / jnp.sum(acc, axis=0, keepdims=True)

    inv_v = total(exp_range(0, 600, max_v) + jnp.where(it8 < 1, e75, 0.0))
    inv_r = total(exp_range(608, 1200, max_r) + jnp.where(it8 >= 1, e75, 0.0) + jnp.where(it8 < 2, e150, 0.0))
    inv_c = total(exp_range(1208, 1232, max_c) + jnp.where(it8 >= 2, e150, 0.0) + jnp.where(it8 < 2, e154, 0.0))
    inv_p = total(jnp.where(in_policy, e154, 0.0))
    hit_v = ints[1:2]
    hit_r = ints[6:7] + BINS
    hit_c = ints[7:8] + 2 * BINS
    counts = jnp.where(in_policy, ints.astype(F32), 0.0)
    share = counts * (rw / jnp.sum(counts, axis=0, keepdims=True))

    def minus(value, lo, *hits):
        at = lax.broadcasted_iota(jnp.int32, value.shape, 0)
        for hit in hits:
            value = value - jnp.where(at == hit - lo, rw, 0.0)
        return value

    d75 = minus(e75 * jnp.where(it8 < 1, inv_v, inv_r), 600, hit_v, hit_r)
    d150 = minus(e150 * jnp.where(it8 < 2, inv_r, inv_c), 1200, hit_r, hit_c)
    d154 = minus(e154 * jnp.where(it8 < 2, inv_c, inv_p), 1232, hit_c) - share
    d154 = jnp.where(it8 < 6, d154, 0.0)

    def emit(lo, hi, inv, hit):
        for r, end in steps(lo, hi, 80):
            dl[r:end, cs] = minus(lg[r:end] * inv, r, hit).astype(BF)

    def pair(first, second):
        return jnp.concatenate([first, second], 0).astype(BF)

    emit(0, 592, inv_v, hit_v)
    dl[592:608, cs] = pair(minus(lg[592:600] * inv_v, 592, hit_v), d75)
    emit(608, 1200, inv_r, hit_r)
    dl[1200:1216, cs] = pair(d150, minus(lg[1208:1216] * inv_c, 1208, hit_c))
    emit(1216, 1232, inv_c, hit_c)
    dl[1232:1248, cs] = pair(d154, jnp.zeros_like(d154))
    dl[1248:HPAD, cs] = jnp.zeros((HPAD - 1248, width), BF)


CB = 256
GROUP = 2


def saved_views(t, mix, xh):
    def mixed(k):
        return mix.at[pl.ds(pl.multiple_of((t * BLOCKS + k - 1) * (D + 16), 16), D + 16)]

    def unit(k):
        return xh.at[pl.ds(pl.multiple_of((t * (BLOCKS + 1) + k) * D, D), D)]

    return mixed, unit


def column_groups(width):
    blocks = [slice(c, c + CB) for c in range(0, width, CB)]
    per = min(GROUP, len(blocks))
    return blocks, per, [slice(c, c + per * CB) for c in range(0, width, per * CB)]


def forward_tower(t, refs, during=None, before_last=None):
    (eye, w, wh, vec, wt, vt, gsb, xt, mix, xh, gp, rstd, stream, mean, ints, width) = refs
    blocks, per, groups = column_groups(width)
    mixed, unit = saved_views(t, mix, xh)
    first_bias = 2 * (BLOCKS + 1)
    ones = jnp.ones((16, D), BF)

    def mean_rows(slot):
        value = nn(ones, wt[slot, 0:D])[0:8] * (1.0 / D)
        high = value.astype(BF).astype(F32)
        wt[slot, D : D + 16] = jnp.concatenate([high, value - high], 0).astype(BF)

    def vectors(k):
        gsb[k % 2] = broadcast_vectors(vt[...], (k, k + BLOCKS + 1)) * ZETA

    def prefetch(k):
        vectors(k)
        row = pl.multiple_of(CAT + jnp.minimum(k - 1, BLOCKS - 1) * D, 32)
        wt[k % 2, 0:D, 0:D] = nt(eye[...], w[t, pl.ds(row, D)]).astype(BF)
        at_row = lax.broadcasted_iota(jnp.int32, (128, 128), 0) == k + first_bias
        at_lane = lax.broadcasted_iota(jnp.int32, (128, 128), 1) == 0
        wt[k % 2, 0:D, D:384] = nn(vt[...], (at_row & at_lane).astype(BF)).astype(BF)
        mean_rows(k % 2)

    def row_of(k):
        return pl.ds(t * (BLOCKS + 1) + k, 1)

    def stage(k, c):
        def keep(rs, a):
            mixed(k)[rs, blocks[c]] = a.astype(BF)

        norm_act(stream, blocks[c], gsb.at[k % 2], unit(k), gp.at[t, k], rstd[row_of(k), blocks[c]], keep)

    def spread(square, k, cs):
        var = jnp.sum(square, axis=0, keepdims=True) * (1.0 / D)
        rstd[row_of(k), cs] = lax.rsqrt(var + 1e-05)

    def add(k, cs, out, fresh):
        shift = out[D : D + 1] + out[D + 8 : D + 9]
        square = jnp.zeros((8, out.shape[1]), F32)
        for r in range(0, D, 32):
            value = out[r : r + 32] - shift
            if not fresh:
                value = stream[r : r + 32, cs] + value
            stream[r : r + 32, cs] = value
            square = square + jnp.sum((value * value).reshape(4, 8, -1), axis=0)
        if not fresh:
            mean[0:1, cs] = mean[0:1, cs] + shift
        spread(square, k + 1, cs)

    def centre(cs):
        total = jnp.zeros((8, CB), F32)
        for r in range(0, D, 32):
            total = total + jnp.sum(stream[r : r + 32, cs].reshape(4, 8, -1), axis=0)
        middle = jnp.sum(total, axis=0, keepdims=True) * (1.0 / D)
        mean[0:1, cs] = middle
        square = jnp.zeros((8, CB), F32)
        for r in range(0, D, 32):
            value = stream[r : r + 32, cs] - middle
            stream[r : r + 32, cs] = value
            square = square + jnp.sum((value * value).reshape(4, 8, -1), axis=0)
        spread(square, 1, cs)

    vt[...] = nt(eye[...], vec[t]).astype(BF)
    vectors(0)
    wt[0, 0:D, 0:D] = nt(eye[...], w[t, 0:D]).astype(BF)
    tile = first_bias // 16 * 16
    picked = lax.broadcasted_iota(jnp.int32, (16, D), 0) == first_bias - tile
    bias = jnp.where(picked, vec[t, tile : tile + 16].astype(F32), 0.0).astype(BF)
    rest = jnp.concatenate([w[t, D:CAT], bias, jnp.zeros((128 - CODES - 16, D), BF)], 0)
    wt[0, 0:D, D:384] = nt(eye[...], rest).astype(BF)
    mean_rows(0)
    for cs in blocks:
        it = lax.broadcasted_iota(jnp.int32, (CODES, CB), 0)
        xt[t, D:CAT, cs] = (it == ints[t, 0:1, cs]).astype(BF)
        xt[t, CAT : CAT + 16, cs] = jnp.ones((16, CB), BF)
    first = [nn(wt[0, :, 0 : CAT + 16], xt[t, :, cs]) for cs in groups]
    prefetch(1)
    for group, cs in enumerate(groups):
        add(-1, cs, first[group], True)
    for cs in blocks:

        def keep(rs, a):
            stream[rs, cs] = a

        norm_act(stream, cs, gsb.at[0], unit(0), gp.at[t, 0], rstd[row_of(0), cs], keep)
        centre(cs)

    def layer(k, more):
        mixed(k)[D : D + 16, :] = jnp.ones((16, width), BF)
        for group, cs in enumerate(groups):
            out = nn(wt[k % 2, :, 0 : D + 16], mixed(k)[:, cs])
            ahead = group + 1 < len(groups)
            if ahead or more:
                for c in range(per):
                    stage(k if ahead else k + 1, (group + 1) % len(groups) * per + c)
            add(k, cs, out, False)
        if more:
            prefetch(k + 2)

    prefetch(2)
    for c in range(per):
        stage(1, c)

    @pl.loop(1, BLOCKS)
    def _(k):
        if during is not None:
            during(k)
        layer(k, True)

    if before_last is not None:
        before_last()
    layer(BLOCKS, False)
    for cs in blocks:
        xt[t + 1, 0:D, cs] = (stream[:, cs] + mean[0:1, cs]).astype(BF)


def backward_tower(t, refs, after_head=None, during=None, before_product=None, after_weights=None):
    (eye, w, wh, vec, wht, vt, gsb, xt, mix, xh, gp, rstd, ds, ex, br, dm, acc, lg, dl, ints, rw, gw, gh, gv, ig, width) = refs
    blocks = [slice(c, c + CB) for c in range(0, width, CB)]
    last = len(blocks) - 1
    mixed, unit = saved_views(t, mix, xh)
    vt[...] = nt(eye[...], vec[t]).astype(BF)
    for h in range(0, HPAD, D):
        wht[h : h + D, :] = nt(eye[...], wh[t, :, h : h + D]).astype(BF)

    def softmax_block(c):
        cs = pl.ds(pl.multiple_of(c * CB, CB), CB)
        lg[...] = nn(wht[...], xt[t + 1, 0:D, cs])
        return cs

    def states_block(c):
        cs = pl.ds(pl.multiple_of(c * CB, CB), CB)
        return cs, nn(wh[t], dl[:, cs])

    def keep_states(cs, product):
        value = product + ex[:, cs]
        ds[:, cs] = value
        br[BLOCKS % 2, :, cs] = value.astype(BF)

    cs = softmax_block(0)
    head_stage(cs, lg, dl, ints[t, :, cs], rw[0:1, cs])

    @pl.loop(1, width // CB)
    def _(c):
        cs = softmax_block(c)
        before, product = states_block(c - 1)
        head_stage(cs, lg, dl, ints[t, :, cs], rw[0:1, cs])
        keep_states(before, product)

    keep_states(*states_block(width // CB - 1))
    for h in range(0, HPAD, D):
        gh[t, :, h : h + D] = nt(xt[t + 1, 0:D, :], dl[h : h + D]).astype(BF)
    if after_head is not None:
        after_head()
    acc[...] = jnp.zeros(acc.shape, F32)
    ones = jnp.ones((16, 128), BF)

    def part(c):
        return dm.at[c * D : c * D + D]

    def gains(k):
        gsb[k % 2, :, 0:128] = broadcast_vectors(vt[...], (k,)) * ZETA

    def row_sums(k):
        for kind in range(2):
            gv[t, kind, pl.ds(k, 1), :] = nt(ones, acc[k % 2, kind].astype(BF))[0:1] * ZETA
        acc[k % 2] = jnp.zeros(acc.shape[1:], F32)

    def product(k, c):
        row = pl.multiple_of(CAT + (k - 1) * D, 32)
        part(c)[...] = nn(w[t, pl.ds(row, D)], br[k % 2, :, blocks[c]])

    def slopes(k, c):
        cs, grad, sums = blocks[c], part(c), acc.at[k % 2]
        s1 = jnp.zeros((8, CB), F32)
        s2 = jnp.zeros((8, CB), F32)
        for r in range(0, D, 32):
            rs = slice(r, r + 32)
            g = wide(gsb[k % 2, rs, 0:128], cs)
            dy = grad[rs, :] * gp[t, k, rs, cs].astype(F32)
            prod = dy * unit(k)[rs, cs].astype(F32)
            back = dy * g
            grad[rs, :] = back
            s1 = s1 + jnp.sum(back.reshape(4, 8, CB), axis=0)
            s2 = s2 + jnp.sum((prod * g).reshape(4, 8, CB), axis=0)
            sums[0, rs] = sums[0, rs] + (prod[:, 0:128] + prod[:, 128:CB])
            sums[1, rs] = sums[1, rs] + (dy[:, 0:128] + dy[:, 128:CB])
        return [jnp.sum(s, axis=0, keepdims=True) * (1.0 / D) for s in (s1, s2)]

    def stage(k, c, first):
        cs = blocks[c]
        means = slopes(k, c)
        scale = rstd[pl.ds(t * (BLOCKS + 1) + k, 1), cs]
        m1, m2 = (jnp.broadcast_to(m * scale, (32, CB)).astype(BF) for m in means)
        for r in range(0, D, 32):
            rs = slice(r, r + 32)
            back = part(c)[rs, :] * scale - (m1 + unit(k)[rs, cs] * m2).astype(F32)
            if first:
                br[0, rs, cs] = back.astype(BF)
            else:
                value = ds[rs, cs] + back
                ds[rs, cs] = value
                br[(k + 1) % 2, rs, cs] = value.astype(BF)

    if before_product is not None:
        before_product()
    gains(BLOCKS)
    gains(BLOCKS - 1)
    product(BLOCKS, 0)

    @pl.loop(0, BLOCKS)
    def _(i):
        k = BLOCKS - i
        if during is not None:
            during(i)
        for c in range(last + 1):
            if c < last:
                product(k, c + 1)
            stage(k, c, False)
            if c == 0:
                full = nt(mixed(k)[...], br[k % 2])
                row = pl.multiple_of(CAT + (k - 1) * D, 32)
                gw[t, pl.ds(row, D), :] = full[0:D].astype(BF)
                gv[t, 2, pl.ds(k, 1), :] = full[D : D + 1]
                product(k - 1, 0)
        gains(k - 2)
        row_sums(k)

    for c, cs in enumerate(blocks):
        part(c)[...] = ds[:, cs]
        stage(0, c, True)
    full = nt(xt[t], br[0])
    gw[t, 0:CAT, :] = full[0:CAT].astype(BF)
    gv[t, 2, 0:1, :] = full[CAT : CAT + 1]
    row_sums(0)
    if after_weights is not None:
        after_weights()
    for cs in blocks:
        back = nn(w[t, 0:D], br[0, :, cs])
        ex[:, cs] = back
        ig[cs, :] = back.T


def compute_kernel(x_ref, ints, rw, w, wh, vec, st, ig, gw, gh, gv, eye, wt, wht, vt, gsb, xt, mix, xh, gp, rstd, mean, stream, ex, br, dm, acc, lg, dl):
    width = x_ref.shape[0]
    eye[...] = identity(D)
    for c in range(0, width, CB):
        cs = slice(c, c + CB)
        xt[0, 0:D, cs] = nt(eye[...], x_ref[cs, :]).astype(BF)
    fwd = (eye, w, wh, vec, wt, vt, gsb, xt, mix, xh, gp, rstd, stream, mean, ints, width)
    @pl.loop(0, 2)
    def _(t):
        forward_tower(t, fwd)

        @pl.loop(0, width // CB)
        def _(c):
            cs = pl.ds(pl.multiple_of(c * CB, CB), CB)
            st[t, cs, :] = nt(eye[...], xt[t + 1, 0:D, cs]).astype(BF)

    ex[...] = jnp.zeros_like(ex)

    @pl.loop(0, 2)
    def _(i):
        t = 1 - i
        backward_tower(
            t,
            (eye, w, wh, vec, wht, vt, gsb, xt, mix, xh, gp, rstd, stream, ex, br, dm, acc, lg, dl, ints, rw, gw, gh, gv, ig.at[t], width),
        )


def work_scratch(width):
    return [
        pltpu.VMEM((D, D), BF),
        pltpu.VMEM((2, D + 16, 384), BF),
        pltpu.VMEM((HPAD, D), BF),
        pltpu.VMEM((D, 128), BF),
        pltpu.VMEM((2, D, 256), F32),
        pltpu.VMEM((3, CAT + 16, width), BF),
        pltpu.VMEM((2 * BLOCKS * (D + 16), width), BF),
        pltpu.VMEM((2 * (BLOCKS + 1) * D, width), BF),
        pltpu.VMEM((2, BLOCKS + 1, D, width), BF),
        pltpu.VMEM((24, width), F32),
        pltpu.VMEM((8, width), F32),
        pltpu.VMEM((D, width), F32),
        pltpu.VMEM((D, width), F32),
        pltpu.VMEM((2, D, width), BF),
        pltpu.VMEM((width // CB * D, CB), F32),
        pltpu.VMEM((2, 2, D, 128), F32),
        pltpu.VMEM((HPAD, CB), F32),
        pltpu.VMEM((HPAD, width), BF),
    ]


def compute(x, ints, rw, w, wh, vec):
    width = x.shape[0]
    vm = pl.BlockSpec(memory_space=pltpu.VMEM)
    return pl.pallas_call(
        compute_kernel,
        out_shape=(
            jax.ShapeDtypeStruct((2, width, D), BF),
            jax.ShapeDtypeStruct((2, width, D), F32),
            jax.ShapeDtypeStruct((2, A_ROWS, D), BF),
            jax.ShapeDtypeStruct((2, D, HPAD), BF),
            jax.ShapeDtypeStruct((2, 3, 16, D), F32),
        ),
        in_specs=[vm] * 6,
        out_specs=(vm,) * 5,
        scratch_shapes=work_scratch(width),
        compiler_params=pltpu.CompilerParams(vmem_limit_bytes=62 * 1024 * 1024),
    )(x, ints, rw, w, wh, vec)


class Plan:
    def __init__(self, n, length):
        self.n, self.length = n, length
        self.rows128 = -(-length // 128)
        block_end, head_end = A_ROWS * D, A_ROWS * D + D * HEADS
        self.a_base, self.a_rows, self.h_first, self.h_rows, self.h_off, self.v_first, self.v_rows, self.v_off = ([] for _ in range(8))
        used = 0
        for i in range(n):
            lo, hi = i * length, (i + 1) * length
            base = min(lo, block_end) // D // 16 * 16
            top = -(-min(hi, block_end) // D)
            a_rows = -(-(top - base) // 16) * 16 if lo < block_end else 0
            first = min(max(lo - block_end, 0), D * HEADS) // HEADS
            last = -(-min(max(hi - block_end, 0), D * HEADS) // HEADS)
            h_rows = last - first if hi > block_end and lo < head_end else 0
            v_first = max(lo - head_end, 0) // D
            v_rows = -(-(hi - head_end) // D) - v_first if hi > head_end else 0
            self.a_base.append(base)
            self.a_rows.append(a_rows)
            self.h_first.append(first)
            self.h_rows.append(h_rows)
            self.h_off.append(a_rows)
            self.v_first.append(v_first)
            self.v_rows.append(v_rows)
            self.v_off.append(a_rows + 5 * h_rows)
            used = max(used, a_rows + 5 * h_rows + v_rows)
        self.heads = max(self.h_rows)
        self.image = (HEADS * self.heads // 128 + 24) // 8 * 8
        self.slot = -(-(used + 1) // 32) * 32

    def at(self, table, me):
        value = jnp.int32(table[0])
        for i in range(1, self.n):
            if table[i] != table[i - 1]:
                value = value + (me >= i).astype(jnp.int32) * (table[i] - table[i - 1])
        return value


MESH = pl.DeviceIdType.MESH


def neighbours(n):
    core = lax.axis_index("tower")
    me = lax.axis_index("dp")
    near_x = me + 1 - 2 * (me % 2)
    near_y = me + 2 - 4 * ((me // 2) % 2)
    return core, me, near_x, near_y


def at(core, index):
    return {"tower": core, "dp": index}


def greet(core, me, near_x, near_y, n, crossed=False):
    barrier = pltpu.get_barrier_semaphore()
    pl.semaphore_signal(barrier, inc=1, device_id=at(1 - core, me), device_id_type=MESH)
    for near in (near_x, near_y, near_x + near_y - me):
        pl.semaphore_signal(barrier, inc=1, device_id=at(core, near), device_id_type=MESH)
    for k in range(1, n // 4):
        pl.semaphore_signal(barrier, inc=1, device_id=at(core, (me + 4 * k) % n), device_id_type=MESH)
    for near in [near_x, near_y] + [(me + 4 * k) % n for k in range(1, n // 4)] if crossed else []:
        pl.semaphore_signal(barrier, inc=1, device_id=at(1 - core, near), device_id_type=MESH)
    return barrier


def place_shard(plan, me, p_ref, slot128, shifted, rolled):
    rows = plan.rows128
    start = me * plan.length
    shift = start % 128
    first = start // 128
    tall = shifted.shape[0]
    height = p_ref.shape[0]
    lane = lax.broadcasted_iota(jnp.int32, (height, 128), 1)
    rolled[0:8] = jnp.zeros((8, 128), F32)
    rolled[8 : 8 + height] = pltpu.roll(p_ref[...], shift, 1)
    shifted[...] = jnp.zeros((tall, 128), F32)
    moved = jnp.where(lane >= shift, rolled[8 : 8 + height], rolled[7 : 7 + height])
    shifted[16 : 16 + height] = moved
    slot128[...] = jnp.zeros(slot128.shape, F32)
    row = lax.broadcasted_iota(jnp.int32, (height, 128), 0)
    base = plan.at(plan.a_base, me)

    @pl.when(plan.at(plan.a_rows, me) > 0)
    def _():
        slot128[pl.ds(first - 2 * base, height)] = jnp.where(row + first < 2 * A_ROWS, moved, 0.0)

    v_start = (A_ROWS * D + D * HEADS) // 128
    v_rows, v_off, v_first = (plan.at(t, me) for t in (plan.v_rows, plan.v_off, plan.v_first))
    tall_v = min(height, -(-2 * max(plan.v_rows) // 8) * 8)

    @pl.when(v_rows > 0)
    def _():
        inside = plan.at([max(0, v_start - i * plan.length // 128) for i in range(plan.n)], me)
        to = 2 * v_off + first + inside - v_start - 2 * v_first
        slot128[pl.ds(to, tall_v)] = shifted[pl.ds(16 + inside, tall_v)]

    h_first, h_rows, h_off = (plan.at(t, me) for t in (plan.h_first, plan.h_rows, plan.h_off))

    @pl.when(h_rows > 0)
    def _():
        tall_h = plan.image
        begin = A_ROWS * D + HEADS * h_first - 128 * first + 128 * 16
        turn = begin % 128
        rolled[0:tall_h] = pltpu.roll(shifted[pl.ds(begin // 128, tall_h)], (128 - turn) % 128, 1)
        rolled[tall_h : tall_h + 8] = jnp.zeros((8, 128), F32)
        lane = lax.broadcasted_iota(jnp.int32, (tall_h, 128), 1)
        shifted[0:tall_h] = jnp.where(lane < 128 - turn, rolled[0:tall_h], rolled[1 : tall_h + 1])
        to = slot128.at[pl.ds(pl.multiple_of(2 * h_off, 8), 10 * plan.heads)]
        it = lax.broadcasted_iota(jnp.int32, (10, 128), 0)
        lane = lax.broadcasted_iota(jnp.int32, (10, 128), 1)
        for k in range(plan.heads):
            row, turn = HEADS * k // 128, HEADS * k % 128
            window = pltpu.roll(shifted[row : row + 16], (128 - turn) % 128, 1)
            value = jnp.where(lane < 128 - turn, window[0:10], window[1:11])
            kept = (it * 128 + lane < HEADS) & (k < h_rows)
            to[10 * k : 10 * k + 10] = to[10 * k : 10 * k + 10] + jnp.where(kept, value, 0.0)


def unpack_rows(plan, i, slot, w, heads, vectors, scratch):
    base, rows = plan.a_base[i], plan.a_rows[i]
    if rows:
        shared = i > 0 and base < plan.a_base[i - 1] + plan.a_rows[i - 1]
        lo = 0
        if shared:
            w[base : base + 16] = w[base : base + 16] + slot[0:16]
            lo = 16
        if rows > lo:
            w[base + lo : base + rows] = slot[lo:rows]
    h_rows, h_off, h_first = plan.h_rows[i], plan.h_off[i], plan.h_first[i]
    v_rows, v_off, v_first = plan.v_rows[i], plan.v_off[i], plan.v_first[i]
    if h_rows or v_rows:
        value = slot.astype(F32)
        scratch[0][...] = value[:, 0:128]
        scratch[1][...] = value[:, 128:D]
    if h_rows:
        shared = i > 0 and plan.h_rows[i - 1] and plan.h_first[i - 1] + plan.h_rows[i - 1] > h_first
        for j in range(5):
            for half in range(2):
                cols = slice(128 * half, 128 * half + 128)
                first = D * j + h_first
                value = scratch[half][pl.ds(h_off + j, h_rows, stride=5)]
                if shared:
                    heads[first : first + 1, cols] = heads[first : first + 1, cols] + value[0:1]
                    if h_rows > 1:
                        heads[first + 1 : first + h_rows, cols] = value[1:h_rows]
                else:
                    heads[first : first + h_rows, cols] = value
    if v_rows:
        shared = v_first and plan.v_first[i - 1] + plan.v_rows[i - 1] > v_first
        shared = shared or (i > 0 and plan.v_rows[i - 1] > 0 and v_first == 0)
        for half in range(2):
            cols = slice(128 * half, 128 * half + 128)
            value = scratch[half][v_off : v_off + v_rows]
            if shared:
                vectors[v_first : v_first + 1, cols] = vectors[v_first : v_first + 1, cols] + value[0:1]
                if v_rows > 1:
                    vectors[v_first + 1 : v_first + v_rows, cols] = value[1:v_rows]
            else:
                vectors[v_first : v_first + v_rows, cols] = value


def split3(value):
    hi = value.astype(BF).astype(F32)
    mid = (value - hi).astype(BF).astype(F32)
    return hi, mid, value - hi - mid


def gather_kernel(plan, p_ref, ints_ref, imp_ref, w, wh, vec, both, rw, slots, slot128, shifted, rolled, scratch, whf, vecf, send, recv):
    n = plan.n
    depth = n // 4
    core, me, near_x, near_y = neighbours(n)
    barrier = greet(core, me, near_x, near_y, n)
    place_shard(plan, me, p_ref, slot128, shifted, rolled)
    pl.semaphore_wait(barrier, depth + 3)
    half = rw.shape[1]
    started = []

    def copy(src, dst, slot, to):
        c = pltpu.make_async_remote_copy(
            src_ref=src, dst_ref=dst, send_sem=send.at[slot], recv_sem=recv.at[slot], device_id=to, device_id_type=MESH
        )
        c.start()
        started.append(c)
        return c

    mine = pl.multiple_of(core * half, half)
    theirs = pl.multiple_of((1 - core) * half, half)
    number = iter(range(1 << 20))
    ints_copy = copy(ints_ref.at[:, pl.ds(theirs, half)], both.at[core], next(number), at(1 - core, me))
    rows = plan.slot
    total = jnp.sum(imp_ref[...].astype(F32), axis=1, keepdims=True)
    lane = lax.broadcasted_iota(jnp.int32, (1, D), 1)
    hi, mid, lo = split3(total)
    left = slot128[pl.ds(0, rows, stride=2)]
    right = slot128[pl.ds(1, rows, stride=2)]
    own = jnp.concatenate([left, right], 1)
    last = jnp.where(lane == 0, hi, jnp.where(lane == 1, mid, jnp.where(lane == 2, lo, 0.0)))
    last_row = lax.broadcasted_iota(jnp.int32, (rows, D), 0) == rows - 1
    slots[core, me] = jnp.where(last_row, last, own).astype(BF)

    def column(index, k):
        return (index + n - 4 * k) % n

    def send_slot(origin, to, lo=0, hi=rows):
        ref = slots.at[core, origin, pl.ds(lo, hi - lo)]
        return copy(ref, ref, next(number), to)

    near_xy = near_x + near_y - me
    cut = rows // 2
    z_in, x_in, y_in, d_in, s_in = {}, {}, {}, {}, []
    for k in sorted(range(1, depth), key=lambda k: (min(k, depth - k), k)):
        z_in[k] = send_slot(me, at(core, (me + 4 * k) % n))
    order = [0] + list(z_in)
    for k in order:
        if k:
            z_in[k].wait_recv()
        x_in[k] = send_slot(column(me, k), at(core, near_x))
        y_in[k] = send_slot(column(me, k), at(core, near_y))
        s_in.append(send_slot(column(me, k), at(1 - core, me)))
    for k in order:
        x_in[k].wait_recv()
        first = send_slot(column(near_x, k), at(core, near_y), 0, cut)
        s_in.append(send_slot(column(near_x, k), at(1 - core, me)))
        y_in[k].wait_recv()
        second = send_slot(column(near_y, k), at(core, near_x), cut, rows)
        s_in.append(send_slot(column(near_y, k), at(1 - core, me)))
        d_in[k] = (first, second)
    for k in order:
        for c in d_in[k]:
            c.wait_recv()
        s_in.append(send_slot(column(near_xy, k), at(1 - core, me)))
    ints_copy.wait_recv()
    both[core] = ints_ref[:, pl.ds(mine, half)]
    for c in s_in:
        c.wait_recv()
    for c in started:
        c.wait_send()
    for t in range(2):
        vecf[...] = jnp.zeros(vecf.shape, F32)
        for i in range(n):
            unpack_rows(plan, i, slots[t, i], w.at[t], whf, vecf, [scratch.at[0], scratch.at[1]])
        for j in range(5):
            wh[t, :, D * j : D * j + D] = whf[D * j : D * j + D].astype(BF)
        vec[t] = vecf[...].astype(BF)
    total = jnp.zeros((1, D), F32)
    for i in range(n):
        tail = slots[0, i, rows - 16 : rows].astype(F32)
        total = total + tail[15:16]
    weight_sum = jnp.sum(jnp.where(lane < 3, total, 0.0), axis=1, keepdims=True)
    rw[...] = jnp.broadcast_to(imp_ref[:, pl.ds(mine, half)].astype(F32) / weight_sum, (8, half))


def gather(plan, p128, ints, imp):
    n, rows = plan.n, plan.slot
    half = ints.shape[1] // 2
    vm = pl.BlockSpec(memory_space=pltpu.VMEM)
    height = p128.shape[0]
    tall = max(2 * rows, height + 40) + 80
    copies = 1 + (n // 4 - 1) + 2 * (n // 4) + 2 * (n // 4) + n
    return pl.pallas_call(
        functools.partial(gather_kernel, plan),
        out_shape=(
            jax.ShapeDtypeStruct((2, A_ROWS, D), BF),
            jax.ShapeDtypeStruct((2, D, HPAD), BF),
            jax.ShapeDtypeStruct((2, 128, D), BF),
            jax.ShapeDtypeStruct((2, 8, half), jnp.int32),
            jax.ShapeDtypeStruct((8, half), F32),
        ),
        in_specs=[vm] * 3,
        out_specs=(vm,) * 5,
        scratch_shapes=[
            pltpu.VMEM((2, n, rows, D), BF),
            pltpu.VMEM((tall, 128), F32),
            pltpu.VMEM((height + 128, 128), F32),
            pltpu.VMEM((height + 40, 128), F32),
            pltpu.VMEM((2, rows, 128), F32),
            pltpu.VMEM((HPAD, D), F32),
            pltpu.VMEM((128, D), F32),
            pltpu.SemaphoreType.DMA((copies,)),
            pltpu.SemaphoreType.DMA((copies,)),
        ],
        compiler_params=pltpu.CompilerParams(
            collective_id=0, has_side_effects=True, vmem_limit_bytes=48 * 1024 * 1024
        ),
    )(p128, ints, imp)


def chunks(height):
    step = max(c for c in range(8, 113, 8) if height % c == 0)
    return [(lo, lo + step) for lo in range(0, height, step)]


def lay_flat(plan, me, slot128, flat, rolled):
    height = rolled.shape[0] - 40
    start = me * plan.length
    shift = start % 128
    first = start // 128
    base = plan.at(plan.a_base, me)
    row = lax.broadcasted_iota(jnp.int32, (height + 8, 128), 0)
    flat[...] = jnp.zeros(flat.shape, F32)

    @pl.when(plan.at(plan.a_rows, me) > 0)
    def _():
        rows = slot128[pl.ds(first - 2 * base, height + 8)]
        flat[16 : 24 + height] = jnp.where(row + first < 2 * A_ROWS, rows, 0.0)

    v_start = (A_ROWS * D + D * HEADS) // 128
    v_rows, v_off, v_first = (plan.at(t, me) for t in (plan.v_rows, plan.v_off, plan.v_first))
    tall_v = min(height, -(-2 * max(plan.v_rows) // 8) * 8)

    @pl.when(v_rows > 0)
    def _():
        inside = plan.at([max(0, v_start - i * plan.length // 128) for i in range(plan.n)], me)
        source = 2 * v_off + first + inside - v_start - 2 * v_first
        to = pl.ds(16 + inside, tall_v)
        flat[to] = flat[to] + slot128[pl.ds(source, tall_v)]

    h_first, h_rows, h_off = (plan.at(t, me) for t in (plan.h_first, plan.h_rows, plan.h_off))

    @pl.when(h_rows > 0)
    def _():
        tall_h = plan.image
        source = slot128.at[pl.ds(pl.multiple_of(2 * h_off, 8), 10 * plan.heads + 6)]
        it = lax.broadcasted_iota(jnp.int32, (16, 128), 0)
        lane = lax.broadcasted_iota(jnp.int32, (16, 128), 1)
        rolled[0 : tall_h + 8] = jnp.zeros((tall_h + 8, 128), F32)
        for k in range(plan.heads):
            row, turn = HEADS * k // 128, HEADS * k % 128
            kept = (it * 128 + lane < HEADS) & (k < h_rows)
            value = pltpu.roll(jnp.where(kept, source[10 * k : 10 * k + 16], 0.0), turn, 1)
            above = jnp.concatenate([jnp.zeros((8, 128), F32), value], 0)[7:23]
            rolled[row : row + 16] = rolled[row : row + 16] + jnp.where(lane >= turn, value, above)
        begin = A_ROWS * D + HEADS * h_first - 128 * first + 128 * 16
        turn = begin % 128
        slot128[0:8] = jnp.zeros((8, 128), F32)
        slot128[8 : 8 + tall_h] = pltpu.roll(rolled[0:tall_h], turn, 1)
        lane = lax.broadcasted_iota(jnp.int32, (tall_h, 128), 1)
        moved = jnp.where(lane >= turn, slot128[8 : 8 + tall_h], slot128[7 : 7 + tall_h])
        to = pl.ds(begin // 128, tall_h)
        flat[to] = flat[to] + moved

    rolled[0 : height + 8] = pltpu.roll(flat[16 : 24 + height], (128 - shift) % 128, 1)
    for lo, hi in chunks(height):
        lane = lax.broadcasted_iota(jnp.int32, (hi - lo, 128), 1)
        flat[lo:hi] = jnp.where(lane < 128 - shift, rolled[lo:hi], rolled[lo + 1 : hi + 1])


def pack_slots(plan, core, gw, gh, gv, rgw, rgh, rgv, slots, sums, vsum, scratch):
    total = gv[core].astype(F32) + rgv[...]
    for kind in range(3):
        vsum[kind * (BLOCKS + 1) : (kind + 1) * (BLOCKS + 1)] = total[kind, 0 : BLOCKS + 1]
    sums[...] = gh[core].astype(F32) + rgh[...].astype(F32)
    for i in range(plan.n):
        base, rows = plan.a_base[i], plan.a_rows[i]
        h_rows, h_off, h_first = plan.h_rows[i], plan.h_off[i], plan.h_first[i]
        v_rows, v_off, v_first = plan.v_rows[i], plan.v_off[i], plan.v_first[i]
        slots[i, rows : plan.slot] = jnp.zeros((plan.slot - rows, D), BF)
        if rows:
            added = gw[core, base : base + rows].astype(F32) + rgw[base : base + rows].astype(F32)
            slots[i, 0:rows] = added.astype(BF)
        if h_rows or v_rows:
            scratch[...] = jnp.zeros(scratch.shape, F32)
            for half in range(2):
                for j in range(5 if h_rows else 0):
                    cols = slice(D * j + 128 * half, D * j + 128 * half + 128)
                    scratch[half, pl.ds(h_off + j, h_rows, stride=5)] = sums[h_first : h_first + h_rows, cols]
                if v_rows:
                    scratch[half, v_off : v_off + v_rows] = vsum[v_first : v_first + v_rows, 128 * half : 128 * half + 128]
            whole = jnp.concatenate([scratch[0], scratch[1]], 1)
            slots[i, rows : plan.slot] = whole[rows:].astype(BF)


def segment_bounds():
    first = [0] + [(CAT + j * D) * D for j in range(BLOCKS + 1)]
    return list(zip(first, first[1:] + [A_ROWS * D + D * HEADS]))


class Rows:
    def __init__(self, ref):
        self.ref, self.height = ref, ref.shape[0]

    def chunks(self):
        return chunks(self.height)

    def get(self, lo, hi):
        return self.ref[lo:hi]

    def put(self, lo, hi, value):
        self.ref[lo:hi] = value


class Flat:
    def __init__(self, ref, buffer):
        self.ref, self.buffer, self.length = ref, buffer, ref.shape[1]
        self.whole = self.length // 1024 * 8
        self.height = -(-self.length // 1024) * 8

    def chunks(self):
        step = next(s for s in range(64, 0, -8) if self.whole % s == 0)
        return [(lo, lo + step) for lo in range(0, self.whole, step)] + [(self.whole, self.height)]

    def ends(self):
        rows = (self.length - 128 * self.whole) // 128
        return rows, self.length % 128, 128 * self.whole, 128 * (self.whole + rows)

    def get(self, lo, hi):
        if hi <= self.whole:
            return self.ref[0:1, 128 * lo : 128 * hi].reshape(hi - lo, 128)
        rows, lanes, first, last = self.ends()
        self.buffer[...] = jnp.zeros((8, 128), F32)
        if rows:
            self.buffer[0:rows] = self.ref[0:1, first:last].reshape(rows, 128)
        if lanes:
            self.buffer[rows : rows + 1, 0:lanes] = self.ref[0:1, last : self.length]
        return self.buffer[...]

    def put(self, lo, hi, value):
        if hi <= self.whole:
            self.ref[0:1, 128 * lo : 128 * hi] = value.reshape(1, 128 * (hi - lo))
            return
        rows, lanes, first, last = self.ends()
        if rows:
            self.ref[0:1, first:last] = value[0:rows].reshape(1, 128 * rows)
        if lanes:
            self.ref[0:1, last : self.length] = value[rows : rows + 1, 0:lanes]


def update_shard(plan, me, p_ref, m_ref, v_ref, outs, flat, squares, sq_in, push, to_plane, to_z):
    first_out, second_out, new_out, norm_out = outs
    height = p_ref.height
    start = me * plan.length
    correction = 1.0 - 0.5**STEP
    bounds = segment_bounds()

    def place(lo, hi):
        shape = (hi - lo, 128)
        return 128 * lo + 128 * lax.broadcasted_iota(jnp.int32, shape, 0) + lax.broadcasted_iota(jnp.int32, shape, 1)

    for lo, hi in p_ref.chunks():
        spot = place(lo, hi)
        grad = jnp.where(spot < plan.length, flat[lo:hi], 0.0)
        first_new = 0.5 * m_ref.get(lo, hi) + 0.5 * grad
        second_new = 0.5 * v_ref.get(lo, hi) + 0.5 * grad * grad
        first_out.put(lo, hi, first_new)
        second_out.put(lo, hi, second_new)
        decay = jnp.where(spot < bounds[-1][1] - start, 0.01 * p_ref.get(lo, hi), 0.0)
        update = first_new / correction / (jnp.sqrt(second_new / correction) + 1e-06) + decay
        flat[lo:hi] = jnp.where(spot < plan.length, update, 0.0)
        new_out.put(lo, hi, p_ref.get(lo, hi) - 0.5 * update)
    squares[...] = jnp.zeros(squares.shape, F32)

    def each_segment(body):
        for j, (first, last) in enumerate(bounds):
            pl.when((first < start + plan.length) & (last > start))(lambda j=j, first=first, last=last: body(j, first, last))

    def square_sums(j, first, last):
        weight, change = jnp.zeros((8, 128), F32), jnp.zeros((8, 128), F32)
        for lo, hi in p_ref.chunks():
            spot = place(lo, hi)
            inside = (spot >= first - start) & (spot < last - start)
            p, u = jnp.where(inside, p_ref.get(lo, hi), 0.0), jnp.where(inside, flat[lo:hi], 0.0)
            weight = weight + jnp.sum((p * p).reshape(-1, 8, 128), axis=0)
            change = change + jnp.sum((u * u).reshape(-1, 8, 128), axis=0)
        squares[0, j : j + 1] = jnp.sum(weight, axis=0, keepdims=True)
        squares[0, 16 + j : 17 + j] = jnp.sum(change, axis=0, keepdims=True)

    each_segment(square_sums)
    total = squares[0]
    for hop, targets in enumerate((to_plane, to_z)):
        lands = range(3) if hop == 0 else range(3, 3 + len(to_z))
        for c in [push(squares.at[hop], sq_in.at[k], to) for k, to in zip(lands, targets)]:
            c.wait_recv()
        for k in lands:
            total = total + sq_in[k]
        squares[hop + 1] = total
    norm = jnp.sqrt(jnp.sum(total, axis=1, keepdims=True))
    squares[3] = jnp.broadcast_to(norm, (32, 128))
    line = jnp.sqrt(jnp.sum(jnp.concatenate([total, jnp.zeros((96, 128), F32)], 0).T, axis=0, keepdims=True))
    norm_out[0:1] = line[:, 0:MATS]
    norm_out[1:2] = pltpu.roll(line, 112, 1)[:, 0:MATS]

    def scaled(j, first, last):
        ratio = squares[3, j : j + 1] / squares[3, 16 + j : 17 + j]
        for lo, hi in p_ref.chunks():
            spot = place(lo, hi)
            inside = (spot >= first - start) & (spot < last - start)
            new_out.put(lo, hi, jnp.where(inside, p_ref.get(lo, hi) - 0.5 * ratio * flat[lo:hi], new_out.get(lo, hi)))

    each_segment(scaled)


def reduce_kernel(
    plan, gw, gh, gv, st, ig, p_ref, m_ref, v_ref,
    st_out, ig_out, first_out, second_out, new_out, norm_out,
    rgw, rgh, rgv, slots, sums, vsum, scratch, in_d, in_x, in_y, in_z, slot128, flat, rolled, squares, sq_in,
    send, recv, local,
):
    n, rows = plan.n, plan.slot
    depth, cut = n // 4, plan.slot // 2
    core, me, near_x, near_y = neighbours(n)
    near_xy = near_x + near_y - me
    barrier = greet(core, me, near_x, near_y, n)
    pl.semaphore_wait(barrier, depth + 3)
    half = st.shape[1]
    number = iter(range(1 << 20))
    started = []

    def copy(src, dst, to):
        slot = next(number)
        c = pltpu.make_async_remote_copy(
            src_ref=src, dst_ref=dst, send_sem=send.at[slot], recv_sem=recv.at[slot], device_id=to, device_id_type=MESH
        )
        c.start()
        started.append(c)
        return c

    def column(index, k):
        return (index + n - 4 * k) % n

    sibling = at(1 - core, me)
    early = [
        copy(gw.at[1 - core], rgw, sibling),
        copy(gh.at[1 - core], rgh, sibling),
        copy(gv.at[1 - core], rgv, sibling),
    ]
    mine = pl.ds(pl.multiple_of(core * half, half), half)
    late = [
        copy(st.at[1 - core], st_out.at[mine], sibling),
        copy(ig.at[1 - core], ig_out.at[mine], sibling),
    ]
    stay = [
        pltpu.make_async_copy(st.at[core], st_out.at[mine], local.at[0]),
        pltpu.make_async_copy(ig.at[core], ig_out.at[mine], local.at[1]),
    ]
    for c in stay:
        c.start()
    for c in early:
        c.wait_recv()
    pack_slots(plan, core, gw, gh, gv, rgw, rgh, rgv, slots, sums, vsum, scratch)
    order = list(range(1, depth)) + [0]
    to_x, to_y = at(core, near_x), at(core, near_y)
    halves = {}
    for k in order:
        diagonal = column(near_xy, k)
        halves[k] = (
            copy(slots.at[diagonal, pl.ds(0, cut)], in_d.at[k, pl.ds(0, cut)], to_y),
            copy(slots.at[diagonal, pl.ds(cut, rows - cut)], in_d.at[k, pl.ds(cut, rows - cut)], to_x),
        )
    fulls = {}
    for k in order:
        ox, oy = column(near_x, k), column(near_y, k)
        halves[k][0].wait_recv()
        slots[ox, 0:cut] = (slots[ox, 0:cut].astype(F32) + in_d[k, 0:cut].astype(F32)).astype(BF)
        first = copy(slots.at[ox], in_x.at[k], to_x)
        halves[k][1].wait_recv()
        slots[oy, cut:rows] = (slots[oy, cut:rows].astype(F32) + in_d[k, cut:rows].astype(F32)).astype(BF)
        fulls[k] = (first, copy(slots.at[oy], in_y.at[k], to_y))
    along = {}
    for k in order:
        own = column(me, k)
        for c in fulls[k]:
            c.wait_recv()
        if k:
            total = slots[own].astype(F32) + in_x[k].astype(F32) + in_y[k].astype(F32)
            slots[own] = total.astype(BF)
            along[k] = copy(slots.at[own], in_z.at[k], at(core, own))
    for c in along.values():
        c.wait_recv()
    total = slots[me].astype(F32) + in_x[0].astype(F32) + in_y[0].astype(F32)
    for k in along:
        total = total + in_z[k].astype(F32)
    slot128[...] = jnp.zeros(slot128.shape, F32)
    slot128[pl.ds(0, rows, stride=2)] = total[:, 0:128]
    slot128[pl.ds(1, rows, stride=2)] = total[:, 128:D]
    lay_flat(plan, me, slot128, flat, rolled)

    to_z = [at(core, column(me, k)) for k in range(1, depth)]
    outs = (Rows(first_out), Rows(second_out), Rows(new_out), norm_out)
    to_plane = [to_x, to_y, at(core, near_xy)]
    update_shard(plan, me, Rows(p_ref), Rows(m_ref), Rows(v_ref), outs, flat, squares, sq_in, copy, to_plane, to_z)
    for c in late:
        c.wait_recv()
    for c in stay:
        c.wait()
    for c in started:
        c.wait_send()


def reduce_and_update(plan, gw, gh, gv, st, ig, p128, m128, v128):
    n, rows = plan.n, plan.slot
    depth = n // 4
    half = st.shape[1]
    height = p128.shape[0]
    vm = pl.BlockSpec(memory_space=pltpu.VMEM)
    hbm = pl.BlockSpec(memory_space=pl.ANY)
    copies = 5 + 2 * depth + 2 * depth + (depth - 1) + (depth - 1) + 3
    flat32 = jax.ShapeDtypeStruct((height, 128), F32)
    return pl.pallas_call(
        functools.partial(reduce_kernel, plan),
        out_shape=(
            jax.ShapeDtypeStruct((2 * half, D), BF),
            jax.ShapeDtypeStruct((2 * half, D), F32),
            flat32,
            flat32,
            flat32,
            jax.ShapeDtypeStruct((2, MATS), F32),
        ),
        in_specs=[vm] * 3 + [hbm] * 2 + [vm] * 3,
        out_specs=(hbm, hbm, vm, vm, vm, vm),
        scratch_shapes=[
            pltpu.VMEM((A_ROWS, D), BF),
            pltpu.VMEM((D, HPAD), BF),
            pltpu.VMEM(gv.shape[1:], F32),
            pltpu.VMEM((n, rows, D), BF),
            pltpu.VMEM((D, HPAD), F32),
            pltpu.VMEM((40, D), F32),
            pltpu.VMEM((2, rows, 128), F32),
            pltpu.VMEM((depth, rows, D), BF),
            pltpu.VMEM((depth, rows, D), BF),
            pltpu.VMEM((depth, rows, D), BF),
            pltpu.VMEM((depth, rows, D), BF),
            pltpu.VMEM((max(2 * rows, height + 48) + 80, 128), F32),
            pltpu.VMEM((height + 128, 128), F32),
            pltpu.VMEM((height + 40, 128), F32),
            pltpu.VMEM((4, 32, 128), F32),
            pltpu.VMEM((2 + depth, 32, 128), F32),
            pltpu.SemaphoreType.DMA((copies,)),
            pltpu.SemaphoreType.DMA((copies,)),
            pltpu.SemaphoreType.DMA((2,)),
        ],
        compiler_params=pltpu.CompilerParams(
            collective_id=1, has_side_effects=True, vmem_limit_bytes=48 * 1024 * 1024
        ),
    )(gw, gh, gv, st, ig, p128, m128, v128)


class Copies:
    def __init__(self, send, recv):
        self.send, self.recv, self.made, self.sent = send, recv, [], set()

    def add(self, src, dst, to, recv_slot=None, only=None):
        self.made.append((src, dst, to, recv_slot, only))
        return len(self.made) - 1

    def get(self, number):
        src, dst, to, recv_slot, _ = self.made[number]
        return pltpu.make_async_remote_copy(
            src_ref=src(), dst_ref=dst(), send_sem=self.send.at[number],
            recv_sem=self.recv.at[number] if recv_slot is None else recv_slot(),
            device_id=to(), device_id_type=MESH,
        )

    def start(self, *numbers):
        for number in numbers:
            self.get(number).start()

    def arrive(self, *numbers):
        for number in numbers:
            self.get(number).wait_recv()

    def leave(self, *numbers):
        for number in numbers:
            only = self.made[number][4]
            if number not in self.sent and only is None:
                self.get(number).wait_send()
            elif number not in self.sent:
                pl.when(only())(lambda number=number: self.get(number).wait_send())
            self.sent.add(number)


def fused_fits(plan):
    depth, half = plan.n // 4, plan.slot // 2
    plain = [b + plan.slot <= A_ROWS for b, h, v in zip(plan.a_base, plan.h_rows, plan.v_rows) if not (h or v)]
    vectors = [rows for rows in plan.v_rows if rows]
    return (
        all(plain)
        and vectors == [3 * (BLOCKS + 1)]
        and plan.n % 4 == 0
        and half >= 32
        and 4 * half <= HPAD
        and 2 * depth * plan.slot <= (BLOCKS + 1) * D
        and depth == 4
        and max(plan.a_rows) <= plan.slot
    )


def train_kernel(
    plan, x_ref, codes_ref, targets_ref, visits_ref, imp_ref, p_ref, m_ref, v_ref,
    st_out, ig_out, first_out, second_out, new_out, norm_out,
    w, wh, vec, both, away, rw, eye, wt, wht, vt, gsb, xt, mix, xh, gp, rstd, mean, stream, ex, br, dm, acc, lg, dl,
    gw, gh, gv, packed, st_stage, slot128, flat, rolled, vsum, vacc, vin, owned, squares, sq_in, tail,
    send, recv, z_recv, own_recv, local, ready,
):
    n, rows = plan.n, plan.slot
    depth, hrows = n // 4, plan.slot // 2
    cut = hrows // 32 * 16
    core, me, near_x, near_y = neighbours(n)
    near_xy = near_x + near_y - me
    width = both.shape[2]
    params_in, first_new, second_new, new = (Flat(ref, tail) for ref in (p_ref, first_out, second_out, new_out))
    moments = [
        pltpu.make_async_copy(src, dst, local.at[3 + i])
        for i, (src, dst) in enumerate(((m_ref, first_out), (v_ref, second_out)))
    ]
    z_me, j_me = me // 4, me % 4
    copies = Copies(send, recv)
    scratch = [slot128.at[0:rows], slot128.at[rows : 2 * rows]]
    barrier = greet(core, me, near_x, near_y, n, True)
    mine = pl.multiple_of(core * width, width)
    theirs = pl.multiple_of((1 - core) * width, width)
    x_copy = pltpu.make_async_copy(x_ref.at[pl.ds(mine, width)], st_stage.at[0], local.at[0])
    x_copy.start()
    for c in moments:
        c.start()
    for to, half in ((both.at[core], mine), (away, theirs)):
        cols = pl.ds(half, width)
        to[0:1] = codes_ref[:, cols]
        to[1:2] = targets_ref[0, :, cols]
        to[2:6] = visits_ref[:, cols]
        to[6:7] = targets_ref[1, :, cols]
        to[7:8] = targets_ref[2, :, cols]
    height = params_in.height
    for lo, hi in params_in.chunks():
        slot128[lo:hi] = params_in.get(lo, hi)
    place_shard(plan, me, slot128.at[0:height], slot128, flat, rolled)

    spare = (BLOCKS + 1) * D

    def slot_part(t, i, lo, count):
        row = pl.multiple_of(spare + rows * (t * depth + i // 4) + lo, 16)
        return xh.at[pl.ds(row, count), pl.ds(pl.multiple_of((i % 4) * D, D), D)]

    def column(index, k):
        return (index + n - 4 * k) % n

    def sibling():
        return at(1 - core, me)

    def same(make, to):
        return copies.add(make, make, to)

    low = core * hrows
    other_low = (1 - core) * hrows
    order = [0] + sorted(range(1, depth), key=lambda k: (min(k, depth - k), k))
    to_x, to_y, to_d = (lambda: at(core, near_x)), (lambda: at(core, near_y)), (lambda: at(core, near_xy))
    swap_ints = copies.add(lambda: away, lambda: both.at[core], sibling)

    def arrival(t, number):
        return own_recv.at[t * (depth + 2) + number]

    own_targets = [(lambda: near_x), (lambda: near_y)] + [lambda k=k: (me + 4 * k) % n for k in order[1:]]
    own_sends = [copies.add(lambda: slot_part(core, me, 0, rows), lambda: slot_part(core, me, 0, rows), sibling, lambda: arrival(core, 0))]
    for number, target in enumerate(own_targets, 1):
        for h in range(2):
            make = lambda h=h: slot_part(core, me, h * hrows, hrows)
            own_sends.append(
                copies.add(make, make, lambda h=h, target=target: at(h, target()), lambda number=number: arrival(core, number))
            )
    own_sends = own_sends[3 + 2 :] + own_sends[1:5] + own_sends[:1]

    def own_arrive(t, number, make):
        pltpu.make_async_remote_copy(
            src_ref=make(), dst_ref=make(), send_sem=send.at[0], recv_sem=arrival(t, number), device_id=sibling(), device_id_type=MESH
        ).wait_recv()

    gathers = []
    for t in range(2):
        g = {}
        for k in order:
            if k:
                g["x", k] = same(lambda t=t, k=k: slot_part(t, column(me, k), low, hrows), to_x)
                g["y", k] = same(lambda t=t, k=k: slot_part(t, column(me, k), low, hrows), to_y)
            g["d", k] = (
                same(lambda t=t, k=k: slot_part(t, column(near_x, k), low, cut), to_y),
                same(lambda t=t, k=k: slot_part(t, column(near_y, k), low + cut, hrows - cut), to_x),
            )
            g["s", k] = [
                same(lambda t=t, k=k, index=index: slot_part(t, column(index, k), low, hrows), sibling) if index is not me or k else None
                for index in (me, near_x, near_y, near_xy)
            ]
        gathers.append(g)

    def gather_0(t):
        pl.when(core == t)(lambda: copies.start(*own_sends))

    def gather_1(t):
        g = gathers[t]
        for number, k in enumerate(order[1:], 3):
            own_arrive(t, number, lambda: slot_part(t, me, low, hrows))
            copies.start(g["x", k], g["y", k], g["s", k][0])

    def gather_2(t):
        g = gathers[t]
        for k in order:
            if k:
                copies.arrive(g["x", k])
            else:
                own_arrive(t, 1, lambda: slot_part(t, me, low, hrows))
            copies.start(g["d", k][0], g["s", k][1])
            if k:
                copies.arrive(g["y", k])
            else:
                own_arrive(t, 2, lambda: slot_part(t, me, low, hrows))
            copies.start(g["d", k][1], g["s", k][2])

    def gather_3(t):
        g = gathers[t]
        for k in order:
            copies.arrive(*g["d", k])
            copies.start(g["s", k][3])

    def gather_4(t):
        g = gathers[t]
        pl.when(core != t)(lambda: own_arrive(t, 0, lambda: slot_part(t, me, 0, rows)))
        for k in order:
            copies.arrive(*(c for c in g["s", k] if c is not None))

    def unpack(t):
        lg[4 * D : 5 * D, 128:D] = jnp.zeros((D, 128), F32)
        vsum[...] = jnp.zeros(vsum.shape, F32)
        for i in range(n):
            row, lane = spare + rows * (t * depth + i // 4), (i % 4) * D
            unpack_rows(plan, i, xh[row : row + rows, lane : lane + D], w.at[t], lg, vsum, scratch)
        for j in range(5):
            wh[t, :, D * j : D * j + D] = lg[D * j : D * j + D].astype(BF)
        vec[t] = vsum[...].astype(BF)

    total = jnp.sum(imp_ref[...].astype(F32), axis=1, keepdims=True)
    lane_d = lax.broadcasted_iota(jnp.int32, (1, D), 1)
    hi, mid, lo = split3(total)
    left = slot128[pl.ds(0, rows, stride=2)]
    right = slot128[pl.ds(1, rows, stride=2)]
    own = jnp.concatenate([left, right], 1)
    last = jnp.where(lane_d == 0, hi, jnp.where(lane_d == 1, mid, jnp.where(lane_d == 2, lo, 0.0)))
    last_row = lax.broadcasted_iota(jnp.int32, (rows, D), 0) == rows - 1
    slot_part(core, me, 0, rows)[...] = jnp.where(last_row, last, own).astype(BF)
    pl.semaphore_wait(barrier, depth + 3 + 2 + depth - 1)
    gather_0(0)
    copies.start(swap_ints)
    eye[...] = identity(D)
    x_copy.wait()
    for c in range(0, width, CB):
        xt[0, 0:D, c : c + CB] = nt(eye[...], st_stage[0, c : c + CB, :]).astype(BF)
    gather_1(0)
    gather_0(1)
    gather_2(0)
    gather_3(0)
    copies.arrive(swap_ints)
    gather_4(0)
    unpack(0)
    total = jnp.zeros((1, D), F32)
    for i in range(n):
        row, lane = spare + rows * (i // 4), (i % 4) * D
        total = total + xh[row + rows - 16 : row + rows, lane : lane + D].astype(F32)[15:16]
    weight_sum = jnp.sum(jnp.where(lane_d < 3, total, 0.0), axis=1, keepdims=True)
    rw[...] = jnp.broadcast_to(imp_ref[:, pl.ds(mine, width)].astype(F32) / weight_sum, (8, width))

    fwd = (eye, w, wh, vec, wt, vt, gsb, xt, mix, xh, gp, rstd, stream, mean, both, width)

    def during_forward(k):
        pl.when(k == 6)(lambda: gather_2(1))

    def emit_states(t):
        for c in range(0, width, CB):
            st_stage[t, c : c + CB, :] = nt(eye[...], xt[t + 1, 0:D, c : c + CB]).astype(BF)

    gather_1(1)
    forward_tower(0, fwd, during_forward, lambda: gather_3(1))
    gather_4(1)
    copies.leave(*range(len(copies.made)))
    unpack(1)
    forward_tower(1, fwd)
    emit_states(0)
    emit_states(1)
    out_rows = pl.ds(mine, width)
    st_copy = copies.add(lambda: st_stage.at[1 - core], lambda: st_out.at[out_rows], sibling)
    copies.start(st_copy)
    st_stay = pltpu.make_async_copy(st_stage.at[core], st_out.at[out_rows], local.at[1])
    st_stay.start()

    packed_of = [i for i in range(n) if plan.h_rows[i] or plan.v_rows[i]]
    owner = plan.v_rows.index(3 * (BLOCKS + 1))

    early = (2, 3)

    def piece(t, zz, b, lo, count):
        if t == 1 and zz in early:
            arena, first, q = dl, 0, 7 * early.index(zz) + b
        elif t == 1:
            arena, first, q = mix, BLOCKS * (D + 16), 7 * zz + b
        else:
            arena, first, q = xh, spare, 7 * zz + b
        row = pl.multiple_of(first + hrows * (q // 4) + lo, 16)
        return arena.at[pl.ds(row, count), pl.ds(pl.multiple_of((q % 4) * D, D), D)]

    def block(t, zz, b):
        return piece(t, zz, b, 0, hrows)

    def z_in(h, k, lo=0, count=hrows):
        return st_stage.at[0, pl.ds(pl.multiple_of(hrows * (h * (depth - 1) + k - 1) + lo, 16), count)]

    def z_out(t, zz, lo, count):
        if t == 1 and zz in early:
            return st_stage.at[1, pl.ds(hrows * early.index(zz) + lo, count)]
        return piece(t, zz, j_me, lo, count)

    def job_pieces(t, zz):
        return [(0, cut), (cut, hrows - cut)] if (t, zz) == (0, 0) else [(0, hrows)]

    def slot_half(t, i, lo):
        if i in packed_of:
            return packed.at[packed_of.index(i), pl.ds(pl.multiple_of(lo, 16), hrows)]
        return gw.at[t, pl.ds(pl.multiple_of(plan.a_base[i] + lo, 16), hrows)]

    j_x, j_y, j_d = near_x % 4, near_y % 4, near_xy % 4
    direct = ((0, 0), (0, 1), (0, 2), (1, 2), (1, 3))
    jobs = {}
    for t in range(2):
        for zz in range(depth):
            job = {}
            job["swap"] = [
                copies.add(lambda t=t, i=4 * zz + j: slot_half(t, i, other_low), lambda t=t, zz=zz, j=j: block(t, zz, j), sibling)
                for j in range(4)
            ]
            pieces = job_pieces(t, zz)
            for side, b, j, to in (("x", 5, j_x, to_x), ("y", 6, j_y, to_y), ("d", 4, j_d, to_d)):
                job[side] = [
                    copies.add(
                        lambda t=t, zz=zz, j=j, lo=lo, count=count: piece(t, zz, j, lo, count),
                        lambda t=t, zz=zz, b=b, lo=lo, count=count: piece(t, zz, b, lo, count),
                        to,
                    )
                    for lo, count in pieces
                    if side != "d" or (t, zz) in direct
                ]
            if (t, zz) not in direct:
                job["d"] = [
                    copies.add(
                        lambda t=t, zz=zz, lo=lo, count=count: piece(t, zz, j_d, lo, count),
                        lambda t=t, zz=zz, lo=lo, count=count: piece(t, zz, 4, lo, count),
                        to,
                    )
                    for to, lo, count in ((to_y, 0, cut), (to_x, cut, hrows - cut))
                ]
            job["z"] = [
                copies.add(
                    lambda t=t, zz=zz, lo=lo, count=count: z_out(t, zz, lo, count),
                    lambda zz=zz, lo=lo, count=count: z_in(core, (zz + depth - z_me) % depth, lo, count),
                    lambda t=t, zz=zz: at(t, 4 * zz + j_me),
                    lambda zz=zz, part=part: z_recv.at[(2 * part + core) * depth + (zz + depth - z_me) % depth],
                    lambda zz=zz: z_me != zz,
                )
                for part, (lo, count) in enumerate(pieces)
            ]
            jobs[t, zz] = job

    def pack(t, planes):
        wanted = [i for i in packed_of if i // 4 in planes]
        for i in wanted:
            a_rows, h_rows, h_off, h_first = plan.a_rows[i], plan.h_rows[i], plan.h_off[i], plan.h_first[i]
            to = packed.at[packed_of.index(i)]
            for part in scratch:
                part[...] = jnp.zeros(part.shape, F32)
            lo16, hi16 = h_first // 16 * 16, -(-(h_first + h_rows) // 16) * 16
            for half in range(2):
                for j in range(5 if h_rows else 0):
                    cols = slice(D * j + 128 * half, D * j + 128 * half + 128)
                    value = gh[t, lo16:hi16, cols].astype(F32)[h_first - lo16 : h_first - lo16 + h_rows]
                    scratch[half][pl.ds(h_off + j, h_rows, stride=5)] = value
            whole = jnp.concatenate([scratch[0][...], scratch[1][...]], 1)
            to[a_rows:rows] = whole[a_rows:].astype(BF)
            if a_rows:
                to[0:a_rows] = gw[t, plan.a_base[i] : plan.a_base[i] + a_rows]

    def plus(*refs):
        value = refs[0][...].astype(F32)
        for ref in refs[1:]:
            value = value + ref[...].astype(F32)
        return value

    def sum_0(t, zz):
        copies.start(*jobs[t, zz]["swap"])

    def sum_1(t, zz):
        job = jobs[t, zz]
        for j in range(4):
            copies.arrive(job["swap"][j])
            target = block(t, zz, j)
            target[...] = plus(slot_half(t, 4 * zz + j, low), target).astype(BF)
        if (t, zz) in direct:
            for x, y, d in zip(job["x"], job["y"], job["d"]):
                copies.start(x, y, d)
        else:
            copies.start(*job["d"])

    def sum_2(t, zz):
        job = jobs[t, zz]
        for side, copy, j, lo, count in (("x", job["d"][0], j_x, 0, cut), ("y", job["d"][1], j_y, cut, hrows - cut)):
            copies.arrive(copy)
            target = piece(t, zz, j, lo, count)
            target[...] = plus(target, piece(t, zz, 4, lo, count)).astype(BF)
            copies.start(*job[side])

    def sum_3(t, zz):
        job = jobs[t, zz]
        pieces = job_pieces(t, zz)
        for part, (lo, count) in enumerate(pieces):
            copies.arrive(job["x"][part], job["y"][part])
            value = plus(*(piece(t, zz, b, lo, count) for b in (j_me, 5, 6)))
            if (t, zz) in direct:
                copies.arrive(job["d"][part])
                value = value + piece(t, zz, 4, lo, count)[...].astype(F32)
            last = part == len(pieces) - 1

            @pl.when(z_me != zz)
            def _():
                z_out(t, zz, lo, count)[...] = value.astype(BF)
                copies.start(job["z"][part])

            @pl.when((z_me == zz) & (core == t))
            def _():
                owned[core, lo : lo + count] = value

            @pl.when((z_me == zz) & (core != t))
            def _():
                owned[2, lo : lo + count] = value
                if last:
                    copies.start(hand_over)

    def z_wait(h, k, part, lo, count):
        src = z_in(h, k, lo, count)
        pltpu.make_async_remote_copy(
            src_ref=src, dst_ref=src, send_sem=send.at[0], recv_sem=z_recv.at[(2 * part + h) * depth + k],
            device_id=sibling(), device_id_type=MESH,
        ).wait_recv()

    def sum_4():
        copies.arrive(hand_over)
        in_pieces = (z_me == 0) & (core == 0)
        for h in range(2):
            for k in range(1, depth):

                @pl.when(in_pieces)
                def _():
                    for part, (lo, count) in enumerate(job_pieces(0, 0)):
                        z_wait(h, k, part, lo, count)

                @pl.when((z_me != 0) | (core != 0))
                def _():
                    z_wait(h, k, 0, 0, hrows)

                final(h)[...] = final(h)[...] + z_in(h, k)[...].astype(F32)

    def final(h):
        return owned.at[h]

    outgo = owned.at[2]

    def vector_step(step):
        sources = [gv.at[1 - core], vacc.at[0], vacc.at[1]]
        along = [lambda k=k: at(core, (me + 4 * k) % n) for k in range(1, depth)]
        targets = [[sibling], [to_x, to_y, to_d], along]
        if step:
            base = gv[core] if step == 1 else vacc[step - 2]
            for number, k in vector_copies[-1]:
                copies.arrive(number)
                base = base + vin[k]
            vacc[step - 1] = base
        if step < 3:
            started = []
            for k, to in enumerate(targets[step], (0, 1, 4)[step]):
                number = copies.add(lambda step=step: sources[step], lambda k=k: vin.at[k], to)
                copies.start(number)
                started.append((number, k))
            vector_copies.append(started)

    vector_copies = []
    hand_over = copies.add(lambda: outgo, lambda: final(core), sibling)
    peers = [(1 - core, me), (core, near_x), (core, near_y), (core, near_xy)] + [(1 - core, (me + 4 * k) % n) for k in range(1, depth)] + [(core, (me + 4 * k) % n) for k in range(1, depth)]

    bwd = (eye, w, wh, vec, wht, vt, gsb, xt, mix, xh, gp, rstd, stream, ex, br, dm, acc, lg, dl, both, rw, gw, gh, gv, dm, width)
    ig_copies = [copies.add(lambda: dm, lambda: ig_out.at[out_rows], sibling, None, lambda t=t: core != t) for t in range(2)]

    def ig_local():
        return pltpu.make_async_copy(dm, ig_out.at[out_rows], local.at[2])

    def emit_inputs(t):
        pl.when(core == t)(lambda: ig_local().start())
        pl.when(core != t)(lambda: copies.start(ig_copies[t]))

    def free_inputs(t):
        pl.when(core == t)(lambda: ig_local().wait())
        pl.when(core != t)(lambda: copies.get(ig_copies[t]).wait_send())

    def signal_ready(which):
        for to_core, to_index in peers:
            pl.semaphore_signal(ready.at[which], inc=1, device_id=at(to_core, to_index), device_id_type=MESH)

    def wait_ready(which):
        pl.semaphore_wait(ready.at[which], len(peers))

    def schedule(i, steps):
        for step in sorted({s[0] for s in steps}):

            def run(step=step):
                for s, f, *args in steps:
                    if s == step:
                        f(*args)

            pl.when(i == step)(run)

    def after_head_1():
        copies.leave(st_copy)
        st_stay.wait()
        signal_ready(0)

    def during_backward_1(i):
        schedule(i, [
            (2, wait_ready, 0), (2, pack, 1, (3,)), (2, sum_0, 1, 3),
            (4, sum_1, 1, 3), (4, pack, 1, (2,)), (4, sum_0, 1, 2),
            (6, sum_1, 1, 2),
            (8, sum_3, 1, 3),
        ])

    ex[...] = jnp.zeros_like(ex)
    backward_tower(1, bwd, after_head_1, during_backward_1, None, lambda: sum_3(1, 2))
    emit_inputs(1)
    signal_ready(1)
    for zz in early:
        job = jobs[1, zz]
        copies.leave(*job["swap"], *job["d"], *job["x"], *job["y"])

    def after_head_0():
        wait_ready(1)
        sum_0(1, 1)
        sum_0(1, 0)
        pack(0, (3,))
        sum_0(0, 3)

    def during_backward_0(i):
        schedule(i, [
            (1, sum_1, 1, 1), (1, sum_1, 1, 0),
            (2, sum_1, 0, 3),
            (4, sum_2, 1, 1), (4, sum_2, 1, 0), (4, pack, 0, (2,)), (4, sum_0, 0, 2),
            (5, sum_2, 0, 3),
            (6, sum_1, 0, 2),
            (8, sum_3, 1, 1), (8, sum_3, 1, 0), (8, sum_0, 0, 1),
            (9, sum_3, 0, 3), (9, sum_1, 0, 1),
        ])

    def after_weights():
        sum_0(0, 0)
        vector_step(0)

    backward_tower(0, bwd, after_head_0, during_backward_0, lambda: free_inputs(1), after_weights)
    emit_inputs(0)
    sum_1(0, 0)
    vector_step(1)
    sum_3(0, 2)
    sum_3(0, 1)
    sum_3(0, 0)
    vector_step(2)
    sum_4()
    vector_step(3)

    slot128[...] = jnp.zeros(slot128.shape, F32)
    for h in range(2):
        slot128[pl.ds(2 * hrows * h, hrows, stride=2)] = final(h)[:, 0:128]
        slot128[pl.ds(2 * hrows * h + 1, hrows, stride=2)] = final(h)[:, 128:D]

    @pl.when(me == owner)
    def _():
        for kind in range(3):
            first = 2 * (plan.v_off[owner] + kind * (BLOCKS + 1))
            for h in range(2):
                value = vacc[2, kind, 0 : BLOCKS + 1, 128 * h : 128 * h + 128]
                slot128[pl.ds(first + h, BLOCKS + 1, stride=2)] = value

    def push(src, dst, to):
        number = copies.add(lambda: src, lambda: dst, lambda: to)
        copies.start(number)
        return copies.get(number)

    lay_flat(plan, me, slot128, flat, rolled)
    for c in moments:
        c.wait()
    update_shard(
        plan, me, params_in, first_new, second_new, (first_new, second_new, new, norm_out),
        flat, squares, sq_in, push, [to_x(), to_y(), to_d()], [at(core, (me + 4 * k) % n) for k in range(1, depth)],
    )
    copies.arrive(st_copy)
    pl.when(core == 0)(lambda: copies.arrive(ig_copies[0]))
    pl.when(core == 1)(lambda: copies.arrive(ig_copies[1]))
    free_inputs(0)
    copies.sent.update(ig_copies)
    assert len(copies.made) <= 11 * n
    copies.leave(*range(len(copies.made)))


def finish_kernel(st, ig, first, second, new, norms, st_out, ig_out, first_out, second_out, new_out, low_out, norms_out, *rest):
    *held, into, outof = rest
    moves = []
    for src, dst, mid, parts in zip((new, ig, st, first, second), (new_out, ig_out, st_out, first_out, second_out), held, (1, 8, 4, 1, 1)):
        rows = src.shape[0] // parts
        for i in range(parts):
            at_rows = pl.ds(i * rows, rows)
            number = len(moves)
            moves.append(
                (
                    pltpu.make_async_copy(src.at[at_rows], mid.at[at_rows], into.at[number]),
                    pltpu.make_async_copy(mid.at[at_rows], dst.at[at_rows], outof.at[number]),
                )
            )
    for load, _ in moves:
        load.start()
    for load, store in moves:
        load.wait()
        store.start()
    size = new.shape[1]
    for lo in range(0, size, 8192):
        hi = min(lo + 8192, size)
        low_out[0:1, lo:hi] = held[0][0:1, lo:hi].astype(BF)
    norms_out[...] = norms[...]
    for _, store in moves:
        store.wait()


def finish(st, ig, first, second, new, norms):
    vm = pl.BlockSpec(memory_space=pltpu.VMEM)
    hbm = pl.BlockSpec(memory_space=pl.ANY)
    arrays = (st, ig, first, second, new)
    shapes = [jax.ShapeDtypeStruct(v.shape, v.dtype) for v in arrays]
    return pl.pallas_call(
        finish_kernel,
        out_shape=(*shapes, jax.ShapeDtypeStruct(new.shape, BF), jax.ShapeDtypeStruct(norms.shape, F32)),
        in_specs=[hbm] * 5 + [vm],
        out_specs=(hbm,) * 5 + (vm,) * 2,
        scratch_shapes=[pltpu.VMEM(v.shape, v.dtype) for v in (new, ig, st, first, second)] + [pltpu.SemaphoreType.DMA((15,))] * 2,
        compiler_params=pltpu.CompilerParams(vmem_limit_bytes=62 * 1024 * 1024),
    )(st, ig, first, second, new, norms)


def train(plan, latent, codes, targets, visits, imp, params, first, second):
    n, rows = plan.n, plan.slot
    depth, hrows = n // 4, rows // 2
    width = codes.shape[1] // 2
    height = -(-params.shape[1] // 1024) * 8
    vm = pl.BlockSpec(memory_space=pltpu.VMEM)
    hbm = pl.BlockSpec(memory_space=pl.ANY)
    packed = sum(1 for h, v in zip(plan.h_rows, plan.v_rows) if h or v)
    return pl.pallas_call(
        functools.partial(train_kernel, plan),
        out_shape=(
            jax.ShapeDtypeStruct((2 * width, D), BF),
            jax.ShapeDtypeStruct((2 * width, D), F32),
            jax.ShapeDtypeStruct(params.shape, F32),
            jax.ShapeDtypeStruct(params.shape, F32),
            jax.ShapeDtypeStruct(params.shape, F32),
            jax.ShapeDtypeStruct((2, MATS), F32),
        ),
        in_specs=[hbm] + [vm] * 5 + [hbm] * 2,
        out_specs=(hbm, hbm, vm, vm, vm, vm),
        scratch_shapes=[
            pltpu.VMEM((2, A_ROWS, D), BF),
            pltpu.VMEM((2, D, HPAD), BF),
            pltpu.VMEM((2, 128, D), BF),
            pltpu.VMEM((2, 8, width), jnp.int32),
            pltpu.VMEM((8, width), jnp.int32),
            pltpu.VMEM((8, width), F32),
            *work_scratch(width),
            pltpu.VMEM((2, A_ROWS, D), BF),
            pltpu.VMEM((2, D, HPAD), BF),
            pltpu.VMEM((2, 3, 16, D), F32),
            pltpu.VMEM((packed, rows, D), BF),
            pltpu.VMEM((2, width, D), BF),
            pltpu.VMEM((max(2 * rows, height + 48) + 80, 128), F32),
            pltpu.VMEM((height + 128, 128), F32),
            pltpu.VMEM((height + 40, 128), F32),
            pltpu.VMEM((128, D), F32),
            pltpu.VMEM((3, 3, 16, D), F32),
            pltpu.VMEM((3 + depth, 3, 16, D), F32),
            pltpu.VMEM((3, hrows, D), F32),
            pltpu.VMEM((4, 32, 128), F32),
            pltpu.VMEM((2 + depth, 32, 128), F32),
            pltpu.VMEM((8, 128), F32),
            pltpu.SemaphoreType.DMA((11 * n,)),
            pltpu.SemaphoreType.DMA((11 * n,)),
            pltpu.SemaphoreType.DMA((4 * depth,)),
            pltpu.SemaphoreType.DMA((2 * (depth + 2),)),
            pltpu.SemaphoreType.DMA((5,)),
            pltpu.SemaphoreType.REGULAR((2,)),
        ],
        compiler_params=pltpu.CompilerParams(
            collective_id=2, has_side_effects=True, vmem_limit_bytes=63 * 1024 * 1024
        ),
    )(latent, codes, targets, visits, imp, params, first, second)


def on_device(latent, codes, targets, visits, importance, params, first_moment, second_moment):
    me = lax.axis_index("tower")
    row_count = latent.shape[0]
    half = row_count // 2
    shard_len = params.shape[1]
    plan = Plan(lax.axis_size("dp"), shard_len)
    if fused_fits(plan):
        states_out, inputs_out, first, second, new, norms = train(
            plan, latent, codes, targets.transpose(1, 0, 2), visits[0].T, importance[None], params, first_moment, second_moment
        )
        states_out, inputs_out, first, second, new, low, norms = finish(states_out, inputs_out, first, second, new, norms)
    else:
        height = -(-plan.rows128 // 8) * 8
        p128, m128, v128 = (
            jnp.pad(v, ((0, 0), (0, 128 * height - shard_len))).reshape(height, 128)
            for v in (params, first_moment, second_moment)
        )
        ints = jnp.concatenate([codes, targets[0, :1], visits[0].T, targets[0, 1:]], 0)
        x = lax.dynamic_slice_in_dim(latent, me * half, half, 0)
        w, wh, vec, both, rw = gather(plan, p128, ints, importance[None])
        st, ig, gw, gh, gv = compute(x, both, rw, w, wh, vec)
        states_out, inputs_out, *flat, norms = reduce_and_update(plan, gw, gh, gv, st, ig, p128, m128, v128)
        first, second, new = (v.reshape(1, -1)[:, :shard_len] for v in flat)
        low = new.astype(BF)
    return (states_out[None], inputs_out[None], first, second, new, low, norms[None])


def solution(mesh):
    in_specs = (
        P("dp", None),
        P("tower", "dp"),
        P("tower", None, "dp"),
        P("tower", "dp", None),
        P("dp"),
        P("tower", "dp"),
        P("tower", "dp"),
        P("tower", "dp"),
    )
    out_specs = (
        P("tower", "dp", None),
        P("tower", "dp", None),
        P("tower", "dp"),
        P("tower", "dp"),
        P("tower", "dp"),
        P("tower", "dp"),
        P("tower", None, None),
    )
    return jax.shard_map(
        on_device, mesh=mesh, in_specs=in_specs, out_specs=out_specs, check_vma=False
    )
```

profile of v0, /device:TPU:0, one launch (start us, length us, event | category | flops | bytes accessed | tf_op | source)
XLA Modules:
  0.0 124.7 jit_solution(15411438740263876612)
XLA Ops:
  0.6 119.0 %shard_map.135 = (bf16[2048,256]{1,0:T(8,128)(2,1)}, f32[2048,256]{1,0:T(8,128)}, f32[1,65904]{1,0:T(1,128)}, f32[1,65904]{1,0:T(1,128)}, f32[1,65904]{1,0:T(1,128)}, /*index=5*/f32[2,12]{1,0:T(2,128)}) custom-call(bf16[2048,256]{1,0:T(8,128)(2,1)} %x_ref.1, s32[1,2048]{1,0:T(1,128)} %codes_ref.1, s32[3,1,2048]{2,1,0:T(1,128)} %bitcast.9, ...), custom_call_target="tpu_custom_call" | custom-call | tf_op jit(solution)/shard_map/pallas_call | solution.py:1741
  119.7 4.9 %shard_map.136 = (bf16[2048,256]{1,0:T(8,128)(2,1)}, f32[2048,256]{1,0:T(8,128)}, f32[1,65904]{1,0:T(1,128)}, f32[1,65904]{1,0:T(1,128)}, f32[1,65904]{1,0:T(1,1...) custom-call(bf16[2048,256]{1,0:T(8,128)(2,1)} %get-tuple-element.20.st, f32[2048,256]{1,0:T(8,128)} %get-tuple-element.21.ig, ...), custom_call_target="tpu_custom_call" | custom-call | tf_op jit(solution)/shard_map/pallas_call | solution.py:1723
where the time goes:
time: 125 us
  Pallas kernels  124 us (99%)
    pallas_call x1, Pallas kernels, train(): pl.pallas_call(functools.partial(train_kernel, plan), out_shape=(jax.Shap...  119 us
    pallas_call x1, Pallas kernels, finish(): pl.pallas_call(finish_kernel, out_shape=(*shapes, jax.ShapeDtypeStruct(ne...  4.91 us

commit v1 on v0

--- a/solution.py
+++ b/solution.py
@@ -1643,9 +1643,9 @@
         vector_step(0)
 
     backward_tower(0, bwd, after_head_0, during_backward_0, lambda: free_inputs(1), after_weights)
-    emit_inputs(0)
     sum_1(0, 0)
     vector_step(1)
+    emit_inputs(0)
     sum_3(0, 2)
     sum_3(0, 1)
     sum_3(0, 0)

time: 125 us -> 125 us (level)
  no operation moved by 1% of the time
where the time goes in v1:
time: 125 us
  Pallas kernels  124 us (99%)
    pallas_call x1, Pallas kernels, train(): pl.pallas_call(functools.partial(train_kernel, plan), out_shape=(jax.Shap...  119 us
    pallas_call x1, Pallas kernels, finish(): pl.pallas_call(finish_kernel, out_shape=(*shapes, jax.ShapeDtypeStruct(ne...  4.91 us

profile of v1, /device:TPU:0, one launch (start us, length us, event | category | flops | bytes accessed | tf_op | source)
XLA Modules:
  0.0 124.7 jit_solution(10096300752295365138)
XLA Ops:
  0.6 119.0 %shard_map.135 = (bf16[2048,256]{1,0:T(8,128)(2,1)}, f32[2048,256]{1,0:T(8,128)}, f32[1,65904]{1,0:T(1,128)}, f32[1,65904]{1,0:T(1,128)}, f32[1,65904]{1,0:T(1,128)}, /*index=5*/f32[2,12]{1,0:T(2,128)}) custom-call(bf16[2048,256]{1,0:T(8,128)(2,1)} %x_ref.1, s32[1,2048]{1,0:T(1,128)} %codes_ref.1, s32[3,1,2048]{2,1,0:T(1,128)} %bitcast.9, ...), custom_call_target="tpu_custom_call" | custom-call | tf_op jit(solution)/shard_map/pallas_call | solution.py:1741
  119.7 4.9 %shard_map.136 = (bf16[2048,256]{1,0:T(8,128)(2,1)}, f32[2048,256]{1,0:T(8,128)}, f32[1,65904]{1,0:T(1,128)}, f32[1,65904]{1,0:T(1,128)}, f32[1,65904]{1,0:T(1,1...) custom-call(bf16[2048,256]{1,0:T(8,128)(2,1)} %get-tuple-element.20.st, f32[2048,256]{1,0:T(8,128)} %get-tuple-element.21.ig, ...), custom_call_target="tpu_custom_call" | custom-call | tf_op jit(solution)/shard_map/pallas_call | solution.py:1723
